TPU v7x, 1024 devices: a whole 4x4x32 slice. The times are simulated.
1024 devices in a mesh: dp: 8 (over x, core), expert: 16 (over z_lo), tensor: 8 (over y, z_hi).
Axes of the slice: x: 4, y: 4, z: 32 (z_hi: 2, z_lo: 16; z = z_hi * 16 + z_lo), core: 2. Of those that a mesh axis runs over, the one named last changes fastest.
Arguments:
- hidden: bfloat16 [8, 16, 768, 1536], P('dp', 'expert'), may hold values from -6 to 6
- out_grad: bfloat16 [8, 16, 768, 4096], P('dp', 'expert', None, 'tensor'), may hold values from -0.119628906 to 0.119628906
- block_list: int32 [8, 16, 6], P('dp', 'expert'), may hold values from 0 to 5, each once within a row
- block_count: int32 [8, 16], P('dp', 'expert'), may hold values from 1 to 6, as said below
- first_moment: float32 [1536, 16, 4096], P('dp', 'expert', 'tensor'), may hold values from -3 to 3
- second_moment: float32 [1536, 16, 4096], P('dp', 'expert', 'tensor'), may hold values from 0.05 to 2
- changed: int32 [8, 16, 8, 12], P('dp', 'expert', 'tensor'), may hold values 0 or 1
- placement: int32 [8, 16, 8, 12, 2], P('dp', 'expert', 'tensor'), may hold values from 0 to 15, all different within a row; in each aligned block of 12 rows (0 to 11, 12 to 23, ..., all dimensions but the last counted through in order) at most 2 rows name the same one
Outputs:
- first_next: float32 [1536, 16, 4096], P('dp', 'expert', 'tensor')
- second_next: float32 [1536, 16, 4096], P('dp', 'expert', 'tensor')
- rollout_inbox: bfloat16 [8, 16, 8, 16, 2, 16, 512], P('dp', 'expert', 'tensor')
Inputs may be any that keep to these rules, and one draw needn't show every extreme that they name: `block_list`: each buffer's list holds each of its 6 blocks once; its first block_count entries are the live blocks. `block_count`: some buffer has all its blocks live. `placement`: the 2 owners of a slice differ; among the slices of one device no owner is named more than 2 times, a bound that some block reaches.
All inputs are finite; a program needn't handle non-finite values. No bound on the sum of `changed` on one device may be relied on, other than what follows from the above.
Results may differ from a plain program's by a relative error of at most 0.0075.
Values may be sent and summed in bfloat16 or wider, within the bound.
A program may use at most 64 MiB of HBM per device.

v0:
```python
import jax
import jax.numpy as jnp
from jax import lax
from jax.sharding import PartitionSpec as P

BLOCK = 128


beta_one = 0.9
beta_two = 0.95
adam_eps = 1e-08
step_number = 50.0


def block_product(running, rows_hidden, rows_grad, block_order, live_count, row_count):

    def add_block(position, partial_value):
        row_start = block_order[position] * BLOCK
        hidden_block = lax.dynamic_slice(rows_hidden, (row_start, 0), (BLOCK, row_count))
        grad_block = lax.dynamic_slice_in_dim(rows_grad, row_start, BLOCK, 0)
        return partial_value + lax.dot_general(
            hidden_block, grad_block, (((0,), (0,)), ((), ())), preferred_element_type=jnp.float32
        )

    return lax.fori_loop(0, live_count, add_block, running)


def slot_targets(owners, capacity):
    entries = owners.shape[0] * owners.shape[1]
    flattened = owners.reshape(entries)
    matching = flattened[:, None] == flattened[None, :]
    earlier = jnp.arange(entries)[None, :] < jnp.arange(entries)[:, None]
    slot_rank = jnp.sum((matching & earlier).astype(jnp.int32), axis=1)
    return (flattened * capacity + slot_rank).reshape(owners.shape)


def on_device(
    hidden, out_grad, block_list, block_count, first_moment, second_moment, changed, placement
):
    rows_hidden = hidden[0, 0]
    rows_grad = out_grad[0, 0]
    block_order = block_list[0, 0]
    live_count = block_count[0, 0]
    n_data = lax.axis_size("dp")
    n_owner = lax.axis_size("expert")
    hidden_rows = rows_hidden.shape[1] // n_data
    feature_cols = rows_grad.shape[1]
    gradient = lax.psum_scatter(
        block_product(
            jnp.zeros((hidden_rows * lax.axis_size("dp"), feature_cols), jnp.float32),
            rows_hidden,
            rows_grad,
            block_order,
            live_count,
            hidden_rows * lax.axis_size("dp"),
        ).astype(jnp.bfloat16),
        "dp",
        scatter_dimension=0,
        tiled=True,
    ).astype(jnp.float32)
    slice_flags = changed[0, 0, 0]
    slices = slice_flags.shape[0]
    changed_rows = (jnp.repeat(slice_flags, hidden_rows // slices) > 0)[:, None, None]
    gradient_rows = gradient[:, None, :]
    m_next = beta_one * first_moment + (1.0 - beta_one) * gradient_rows
    v_next = beta_two * second_moment + (1.0 - beta_two) * gradient_rows * gradient_rows
    corr_one = 1.0 - beta_one**step_number
    corr_two = 1.0 - beta_two**step_number
    update = m_next / corr_one / (jnp.sqrt(v_next / corr_two) + adam_eps)
    first_next = jnp.where(changed_rows, m_next, first_moment)
    second_next = jnp.where(changed_rows, v_next, second_moment)
    update = jnp.where(changed_rows, update, 0.0).astype(jnp.bfloat16)
    owners = placement[0, 0, 0]
    copies = owners.shape[1]
    capacity = max(2, slices * copies * 4 // (3 * n_owner))
    targets = slot_targets(owners, capacity)
    choose = jnp.sum(
        (jnp.arange(n_owner * capacity)[:, None, None] == targets[None]).astype(jnp.int32), axis=2
    )
    choose = choose.astype(jnp.bfloat16)
    flat_update = update.reshape(slices, -1)
    outgoing = jnp.dot(choose, flat_update, preferred_element_type=jnp.float32).astype(jnp.bfloat16)
    outgoing = outgoing.reshape(n_owner, capacity, hidden_rows // slices, feature_cols)
    received = lax.all_to_all(outgoing, "expert", split_axis=0, concat_axis=0, tiled=True)
    return (first_next, second_next, received[None, None, None])


def solution(mesh):
    return jax.shard_map(
        on_device,
        mesh=mesh,
        in_specs=(
            P("dp", "expert", None, None),
            P("dp", "expert", None, "tensor"),
            P("dp", "expert", None),
            P("dp", "expert"),
            P("dp", "expert", "tensor"),
            P("dp", "expert", "tensor"),
            P("dp", "expert", "tensor", None),
            P("dp", "expert", "tensor", None, None),
        ),
        out_specs=(
            P("dp", "expert", "tensor"),
            P("dp", "expert", "tensor"),
            P("dp", "expert", "tensor", None, None, None, None),
        ),
        check_vma=False,
    )
```

profile of v0, /device:TPU:8, one launch (start us, length us, event | category | flops | bytes accessed | tf_op | source)
XLA Modules:
  0.0 172.8 jit_solution(10414402516168815838)
XLA Ops:
  7.2 0.0 copy-start.3
  7.2 0.0 reduce-scatter.2.cloned.1.call-start
  7.2 0.4 broadcast_in_dim.37
  7.6 0.2 copy-done.3
  7.8 14.8 %while.10 = (s32[]{:T(128)}, f32[1536,512]{1,0:T(8,128)S(1)}, s32[]{:T(128)}, s32[6]{0:T(128)S(1)}, bf16[768,1536]{1,0:T(8,128)(2,1)}, /*index=5*/bf16[768,512]{...) while((s32[]{:T(128)}, f32[1536,512]{1,0:T(8,128)S(1)}, s32[]{:T(128)}, ...), condition=%wide.region_1.0_spmd, body=%wide.region_0.0_spmd.sunk | while | flops 202113024 | bytes 6816969 | solution.py:25
  8.5 0.6 dynamic_slice.18
  9.7 1.6 convolution_add_fusion.2
  12.0 0.6 dynamic_slice.18
  13.3 1.6 convolution_add_fusion.2
  15.6 0.6 dynamic_slice.18
  16.8 1.6 convolution_add_fusion.2
  19.1 0.6 dynamic_slice.18
  20.4 1.6 convolution_add_fusion.2
  22.7 0.0 copy-start.4
  22.7 0.0 copy-start.2
  22.7 0.0 copy-start
  22.7 1.4 convert_element_type.21
  24.1 0.0 reduce-scatter.2.cloned.1.call-update
  24.1 0.0 copy-done.4
  24.1 0.0 copy-start.1
  24.1 0.1 broadcast_in_dim.35
  24.2 0.1 gt.20
  24.3 0.0 copy-done.2
  24.3 0.1 copy.20
  24.4 0.1 eq.29
  24.5 0.2 convert_reduce_fusion.1
  24.6 0.1 reduce_sum.21
  24.7 0.1 copy.21
  24.8 0.1 copy.22
  24.9 0.1 fusion.4
  25.0 60.2 %reduce-scatter.2.cloned.1.call-done = bf16[192,512]{1,0:T(8,128)(2,1)} async-done(((bf16[1536,512]{1,0:T(8,128)(2,1)}), bf16[192,512]{1,0:T(8,128)(2,1)}) %reduce-scatter.2.cloned.1.call-update) | async-done | bytes 196624 | tf_op jit(solution)/shard_map/reduce_scatter | solution.py:48
  85.2 1.0 fusion.3
  86.3 0.0 copy-done
  86.3 5.0 %convert_reduce_fusion = bf16[192,512]{1,0:T(8,128)(2,1)S(1)} fusion(pred[192]{0:T(512)(128)(4,1)S(1)} %gt.20, f32[192,512]{1,0:T(8,128)S(1)} %get-tuple-element.50, f32[192,1,512]{2,1,0:T(1,128)} %param.14, f32[192,1,512]{2,0,1:T(8,128)S(1)} %get-tuple-element.49, f32[192,1,512]{2,1,0:T(1,128)S(1)} %copy-done), kind=kLoop, calls=%fused_computation.12 | loop fusion | flops 983040 | bytes 1769664 | tf_op jit(solution)/shard_map/convert_element_type | solution.py:72
  91.3 0.1 reshape.43
  91.4 0.3 convolution_convert_fusion
  91.7 1.0 copy.23
  92.7 20.4 %all-to-all-start = ((bf16[16,2,16,512]{3,2,1,0:T(8,128)(2,1)}), bf16[16,2,16,512]{3,2,1,0:T(8,128)(2,1)S(1)}, u32[]{:S(2)}, u32[]{:S(2)}) async-start(bf16[16,2,16,512]{3,2,1,0:T(8,128)(2,1)} %bitcast.11), calls=%async_computation.1 | async-start | bytes 1048576 | tf_op jit(solution)/shard_map/all_to_all | solution.py:84
  113.1 0.0 copy-done.1
  113.1 2.8 %broadcast_select_fusion.1 = (f32[192,1,512]{2,1,0:T(1,128)}, f32[192,1,512]{2,1,0:T(1,128)}) fusion(f32[192,1,512]{2,1,0:T(1,128)S(1)} %copy-done, pred[192]{0:T(512)(128)(4,1)S(1)} %gt.20, f32[192,1,512]{2,0,1:T(8,128)S(1)} %get-tuple-element.49, f32[192,1,512]{2,1,0:T(1,128)S(1)} %copy-done.1, f32[192,512]{1,0:T(8,128)S(1)} %get-tuple-element.50), kind=kLoop, calls=%fused_computation.6 | loop fusion | flops 589824 | bytes 2359488 | tf_op jit(solution)/shard_map/jit(_where)/select_n | solution.py:71
  116.0 49.2 %all-to-all-done = bf16[16,2,16,512]{3,2,1,0:T(8,128)(2,1)S(1)} async-done(((bf16[16,2,16,512]{3,2,1,0:T(8,128)(2,1)}), bf16[16,2,16,512]{3,2,1,0:T(8,128)(2,1)S(1)}, u32[]{:S(2)}, u32[]{:S(2)}) %all-to-all-start) | async-done | bytes 524320 | tf_op jit(solution)/shard_map/all_to_all | solution.py:84
  165.2 0.8 copy.36
  (2 shorter events, 0.0 us)
Async XLA Ops:
  7.2 0.7 copy-start.3
  7.2 78.1 %reduce-scatter.2.cloned.1.call-start = ((), (), s32[]{:S(2)}) async-start(), calls=%async_computation.2 | async-start | bytes 1769472 | tf_op jit(solution)/shard_map/reduce_scatter | solution.py:48
  22.7 1.4 copy-start.4
  22.7 1.6 copy-start.2
  22.7 63.6 %copy-start = (f32[192,1,512]{2,1,0:T(1,128)S(1)}, f32[192,1,512]{2,1,0:T(1,128)}, u32[]{:S(2)}) copy-start(f32[192,1,512]{2,1,0:T(1,128)} %param.15) | copy-start | bytes 1179652
  24.1 89.0 %copy-start.1 = (f32[192,1,512]{2,1,0:T(1,128)S(1)}, f32[192,1,512]{2,1,0:T(1,128)}, u32[]{:S(2)}) copy-start(f32[192,1,512]{2,1,0:T(1,128)} %param.14) | copy-start | bytes 1179652
  92.7 72.5 %all-to-all-start = ((bf16[16,2,16,512]{3,2,1,0:T(8,128)(2,1)}), bf16[16,2,16,512]{3,2,1,0:T(8,128)(2,1)S(1)}, u32[]{:S(2)}, u32[]{:S(2)}) async-start(bf16[16,2,16,512]{3,2,1,0:T(8,128)(2,1)} %bitcast.11), calls=%async_computation.1 | async-start | bytes 1048576 | tf_op jit(solution)/shard_map/all_to_all | solution.py:84
Sparse Core Ops, SparseCore 0:
  24.2 60.9 reduce-scatter.1
where the time goes:
time: 174 us; the launch traced here: 173 us
  waiting for transfers between devices  109 us (63%)
  starting transfers between devices  20.5 us (12%)
  between operations  14.2 us (8%)
  other arithmetic  10.5 us (6%)
  matrix products  6.83 us (4%)
  loops' own time  5.97 us (3%)
  local copies, waits for them, and re-layouts  5.48 us (3%)
    reduce_scatter x1, waiting for transfers between devices, on_device(): lax.psum_scatter(block_product(jnp.zeros((hidden_rows * lax.axis_size('dp...  60.2 us
    all_to_all x1, waiting for transfers between devices, on_device(): lax.all_to_all(outgoing, 'expert', split_axis=0, concat_axis=0, tiled=True)  49.2 us
    all_to_all x1, starting transfers between devices, on_device(): lax.all_to_all(outgoing, 'expert', split_axis=0, concat_axis=0, tiled=True)  20.4 us
    dot_general x4, matrix products, add_block(): lax.dot_general(hidden_block, grad_block, (((0,), (0,)), ((), ())), prefe...  6.52 us
    another operation x1, loops' own time, block_product(): return lax.fori_loop(0, live_count, add_block, running)  5.97 us
    convert_element_type x1, other arithmetic, on_device(): update = jnp.where(changed_rows, update, 0.0).astype(jnp.bfloat16)  4.99 us
  transfers between devices with their start and end apart: 2, of which 2 were waited for; matrix products, arithmetic and copies ran while one was open for 2% of the time, Pallas kernels for 0%

commit v1 on v0

v1 whole, which is shorter than its diff:
```python
import functools

import jax
import jax.numpy as jnp
from jax import lax
from jax.experimental import pallas as pl
from jax.experimental.pallas import tpu as pltpu
from jax.sharding import PartitionSpec as P

MESH = pl.DeviceIdType.MESH
BLOCK = 128
LANES = 128
SLOTS = 2
STRIDE = 5

beta_one = 0.9
beta_two = 0.95
adam_eps = 1e-08
step_number = 50.0


def kernel(
    n_dp,
    n_exp,
    slices,
    hidden,
    out_grad,
    block_list,
    block_count,
    first,
    second,
    changed,
    placement,
    first_out,
    second_out,
    inbox,
    h_buf,
    g_buf,
    ht_buf,
    m_buf,
    v_buf,
    keep_buf,
    part,
    part_in,
    upd,
    pack,
    pack_in,
    idx_vec,
    idx,
    load_sem,
    idx_sem,
    rs_send,
    rs_recv,
    z_send,
    z_recv,
    near,
    relay_left,
    relay_right,
):
    dp = lax.axis_index("dp")
    me = lax.axis_index("expert")
    tokens, hidden_all = h_buf.shape
    rows = hidden_all // n_dp
    slice_rows = rows // slices
    chunks = g_buf.shape[1] // LANES
    blocks = tokens // BLOCK

    barrier = pltpu.get_barrier_semaphore()
    for off in range(1, n_dp):
        pl.semaphore_signal(
            barrier, inc=1, device_id={"dp": lax.rem(dp + off, n_dp)}, device_id_type=MESH
        )
    for off in range(1, STRIDE + 1):

        @pl.when(me + off < n_exp)
        def _():
            pl.semaphore_signal(
                barrier, inc=1, device_id={"expert": me + off}, device_id_type=MESH
            )

    groups = hidden_all // 512
    loads = [pltpu.make_async_copy(out_grad.at[0, 0], g_buf, load_sem.at[0])]
    for i in range(groups):
        cols = pl.ds(i * 512, 512)
        loads.append(
            pltpu.make_async_copy(hidden.at[0, 0, :, cols], h_buf.at[:, cols], load_sem.at[1 + i])
        )
    loads.append(pltpu.make_async_copy(first, m_buf, load_sem.at[1 + groups]))
    loads.append(pltpu.make_async_copy(second, v_buf, load_sem.at[2 + groups]))
    for cp in loads:
        cp.start()

    lane = lax.broadcasted_iota(jnp.int32, (8, LANES), 1)
    owner_of = lane // SLOTS
    slot_of = lane - owner_of * SLOTS
    count = jnp.zeros((8, LANES), jnp.int32)
    table = jnp.full((8, LANES), slices, jnp.int32)
    for s in range(slices):
        value = jnp.where(changed[0, 0, 0, s] > 0, s, slices)
        for k in range(2):
            hit = owner_of == placement[0, 0, 0, k, s]
            table = jnp.where(hit & (count == slot_of), value, table)
            count = count + hit.astype(jnp.int32)
    idx_vec[...] = table
    idx_copy = pltpu.make_async_copy(idx_vec, idx, idx_sem)
    idx_copy.start()
    for s in range(slices):
        keep_buf[pl.ds(s * slice_rows, slice_rows), :] = jnp.full(
            (slice_rows, LANES), changed[0, 0, 0, s], jnp.int32
        )
    upd[slices] = jnp.zeros(upd.shape[1:], upd.dtype)

    loads[0].wait()
    for b in range(blocks):
        live = jnp.int32(0)
        for j in range(blocks):
            hit = (block_list[0, 0, j] == b) & (block_count[0, 0] > j)
            live = live | hit.astype(jnp.int32)
        at = pl.ds(b * BLOCK, BLOCK)
        block = g_buf[at, :]
        g_buf[at, :] = jnp.where(live > 0, block, jnp.zeros_like(block))
    for i in range(groups):
        loads[1 + i].wait()
        for j in range(512 // LANES):
            at = i * 512 + j * LANES
            ht_buf[pl.ds(at, LANES), :] = h_buf[:, pl.ds(at, LANES)].T

    def reduce_copy(c, peer, slot):
        return pltpu.make_async_remote_copy(
            src_ref=part.at[c, peer],
            dst_ref=part_in.at[c, slot],
            send_sem=rs_send.at[c, peer],
            recv_sem=rs_recv.at[c, slot],
            device_id={"dp": peer},
            device_id_type=MESH,
        )

    for c in range(chunks):
        for d in range(n_dp):
            prod = jnp.dot(
                ht_buf[pl.ds(d * rows, rows), :],
                g_buf[:, pl.ds(c * LANES, LANES)],
                preferred_element_type=jnp.float32,
            )
            part[c, d] = prod.astype(part.dtype)
        if c == 0:
            pl.semaphore_wait(barrier, n_dp - 1 + jnp.minimum(me, STRIDE))
            for off in range(1, STRIDE + 1):

                @pl.when(me - off >= 0)
                def _():
                    pl.semaphore_signal(
                        near, inc=1, device_id={"expert": me - off}, device_id_type=MESH
                    )
        for off in range(1, n_dp):
            reduce_copy(c, lax.rem(dp + off, n_dp), dp).start()

    loads[1 + groups].wait()
    loads[2 + groups].wait()
    idx_copy.wait()

    def tell(sem, peer):
        pl.semaphore_signal(sem, inc=1, device_id={"expert": peer}, device_id_type=MESH)

    @pl.when(me + 1 < n_exp)
    def _():
        pl.semaphore_wait(near, jnp.minimum(n_exp - 1 - me, STRIDE))

    @pl.when((me + STRIDE < n_exp) & (me > 0))
    def _():
        tell(relay_left.at[0], me + STRIDE)

    @pl.when((me - STRIDE >= 0) & (me + 1 < n_exp))
    def _():
        tell(relay_right.at[0], me - STRIDE)

    hops = -(-(n_exp - 1) // STRIDE) - 1

    def learn(sems, reach, onward, far_enough):
        for h in range(hops):

            @pl.when(reach > (h + 1) * STRIDE)
            def _():
                pl.semaphore_wait(sems.at[h], 1)

            if h + 1 < hops:

                @pl.when(far_enough & (reach > (h + 1) * STRIDE))
                def _():
                    tell(sems.at[h + 1], onward)

    def route_copy(c, peer, slot):
        return pltpu.make_async_remote_copy(
            src_ref=pack.at[c, peer],
            dst_ref=pack_in.at[c, slot],
            send_sem=z_send.at[c, peer],
            recv_sem=z_recv.at[c, slot],
            device_id={"expert": peer},
            device_id_type=MESH,
        )

    corr_one = 1.0 - beta_one**step_number
    corr_two = 1.0 - beta_two**step_number
    for c in range(chunks):
        total = part[c, dp].astype(jnp.float32)
        for off in range(1, n_dp):
            peer = lax.rem(dp + off, n_dp)
            reduce_copy(c, peer, peer).wait_recv()
            total = total + part_in[c, peer].astype(jnp.float32)
        at = pl.ds(c, rows, stride=chunks)
        m_old = m_buf[at, :]
        v_old = v_buf[at, :]
        keep = keep_buf[...] > 0
        m_next = beta_one * m_old + (1.0 - beta_one) * total
        v_next = beta_two * v_old + (1.0 - beta_two) * total * total
        update = m_next / corr_one / (jnp.sqrt(v_next / corr_two) + adam_eps)
        first_out[at, :] = jnp.where(keep, m_next, m_old)
        second_out[at, :] = jnp.where(keep, v_next, v_old)
        upd[pl.ds(0, slices)] = update.astype(upd.dtype).reshape(slices, slice_rows, LANES)
        for n in range(n_exp * SLOTS):
            pack[c, n // SLOTS, n % SLOTS] = upd[idx[0, n]]
        if c == 0:
            learn(relay_left, me, me + STRIDE, me + STRIDE < n_exp)

        @pl.loop(0, n_exp - 1)
        def _(i):
            @pl.when(i < me)
            def _():
                route_copy(c, i, me).start()

        @pl.loop(1, STRIDE + 1)
        def _(off):
            @pl.when(me + off < n_exp)
            def _():
                route_copy(c, me + off, me).start()

        if c == 0:
            learn(relay_right, n_exp - 1 - me, me - STRIDE, me - STRIDE >= 0)

        @pl.loop(STRIDE + 1, n_exp)
        def _(off):
            @pl.when(me + off < n_exp)
            def _():
                route_copy(c, me + off, me).start()

    for c in range(chunks):
        cols = pl.ds(c * LANES, LANES)
        inbox[me, :, :, cols] = pack[c, me]

        @pl.loop(1, n_exp)
        def _(off):
            peer = lax.rem(me + off, n_exp)
            route_copy(c, peer, peer).wait_recv()
            inbox[peer, :, :, cols] = pack_in[c, peer]

    for c in range(chunks):
        for off in range(1, n_dp):
            reduce_copy(c, lax.rem(dp + off, n_dp), dp).wait_send()

        @pl.loop(1, n_exp)
        def _(off):
            route_copy(c, lax.rem(me + off, n_exp), me).wait_send()


def on_device(
    hidden, out_grad, block_list, block_count, first_moment, second_moment, changed, placement
):
    n_dp = lax.axis_size("dp")
    n_exp = lax.axis_size("expert")
    tokens, hidden_all = hidden.shape[2:]
    features = out_grad.shape[3]
    slices = changed.shape[3]
    rows = first_moment.shape[0]
    slice_rows = rows // slices
    chunks = features // LANES
    flat = (rows * chunks, LANES)
    f32, bf16 = jnp.float32, jnp.bfloat16
    any_spec = pl.BlockSpec(memory_space=pltpu.HBM)
    smem = pl.BlockSpec(memory_space=pltpu.SMEM)
    vmem = pl.BlockSpec(memory_space=pltpu.VMEM)
    dma = pltpu.SemaphoreType.DMA
    regular = pltpu.SemaphoreType.REGULAR
    first_next, second_next, inbox = pl.pallas_call(
        functools.partial(kernel, n_dp, n_exp, slices),
        out_shape=(
            jax.ShapeDtypeStruct(flat, f32),
            jax.ShapeDtypeStruct(flat, f32),
            jax.ShapeDtypeStruct((n_exp, SLOTS, slice_rows, features), bf16),
        ),
        in_specs=[any_spec, any_spec, smem, smem, any_spec, any_spec, smem, smem],
        out_specs=(vmem, vmem, vmem),
        scratch_shapes=[
            pltpu.VMEM((tokens, hidden_all), bf16),
            pltpu.VMEM((tokens, features), bf16),
            pltpu.VMEM((hidden_all, tokens), bf16),
            pltpu.VMEM(flat, f32),
            pltpu.VMEM(flat, f32),
            pltpu.VMEM((rows, LANES), jnp.int32),
            pltpu.VMEM((chunks, n_dp, rows, LANES), bf16),
            pltpu.VMEM((chunks, n_dp, rows, LANES), bf16),
            pltpu.VMEM((slices + 1, slice_rows, LANES), bf16),
            pltpu.VMEM((chunks, n_exp, SLOTS, slice_rows, LANES), bf16),
            pltpu.VMEM((chunks, n_exp, SLOTS, slice_rows, LANES), bf16),
            pltpu.VMEM((8, LANES), jnp.int32),
            pltpu.SMEM((8, LANES), jnp.int32),
            dma((3 + hidden_all // 512,)),
            dma(()),
            dma((chunks, n_dp)),
            dma((chunks, n_dp)),
            dma((chunks, n_exp)),
            dma((chunks, n_exp)),
            regular(()),
            regular((4,)),
            regular((4,)),
        ],
        compiler_params=pltpu.CompilerParams(
            collective_id=0, has_side_effects=True, vmem_limit_bytes=60 << 20
        ),
    )(
        hidden,
        out_grad,
        block_list,
        block_count,
        first_moment.reshape(flat),
        second_moment.reshape(flat),
        changed,
        jnp.swapaxes(placement, 3, 4),
    )
    shape = first_moment.shape
    return (
        first_next.reshape(shape),
        second_next.reshape(shape),
        inbox[None, None, None],
    )


def solution(mesh):
    return jax.shard_map(
        on_device,
        mesh=mesh,
        in_specs=(
            P("dp", "expert", None, None),
            P("dp", "expert", None, "tensor"),
            P("dp", "expert", None),
            P("dp", "expert"),
            P("dp", "expert", "tensor"),
            P("dp", "expert", "tensor"),
            P("dp", "expert", "tensor", None),
            P("dp", "expert", "tensor", None, None),
        ),
        out_specs=(
            P("dp", "expert", "tensor"),
            P("dp", "expert", "tensor"),
            P("dp", "expert", "tensor", None, None, None, None),
        ),
        check_vma=False,
    )
```

time: 174 us -> 84.4 us (0.49)
  the two profiles are of different devices: /device:TPU:8 before, /device:TPU:1 now
where the time goes in v1:
time: 84.4 us; the launch traced here: 84.1 us
  Pallas kernels  76.9 us (91%)
  local copies, waits for them, and re-layouts  5.9 us (7%)
  between operations  1.29 us (2%)
    pallas_call x1, Pallas kernels, on_device(): pl.pallas_call(functools.partial(kernel, n_dp, n_exp, slices), out_shape=...  76.9 us
    unnamed x3, local copies, waits for them, and re-layouts  5.9 us

profile of v1, /device:TPU:1, one launch (start us, length us, event | category | flops | bytes accessed | tf_op | source)
XLA Modules:
  0.0 84.1 jit_solution(6940029883799355560)
XLA Ops:
  1.3 76.9 %shard_map.103 = (f32[768,128]{1,0:T(8,128)}, f32[768,128]{1,0:T(8,128)}, bf16[16,2,16,512]{3,2,1,0:T(8,128)(2,1)}) custom-call(bf16[1,1,768,1536]{3,2,1,0:T(8,128)(2,1)} %hidden.1, bf16[1,1,768,512]{3,2,1,0:T(8,128)(2,1)} %out_grad.1, s32[1,1,6]{2,1,0:T(1,128)} %block_list.1, s32[1,1]{1,0:T(1,128)S(6)} %copy.16.block_count, f32[768,128]{1,0:T(8,128)} %bitcast.9, ...), custom_call_target="tpu_custom_call" | custom-call | tf_op jit(solution)/shard_map/pallas_call | solution.py:283
  78.2 2.0 %copy.17 = f32[192,1,512]{2,1,0:T(1,128)} copy(f32[192,1,512]{2,1,0:T(1,128)} %bitcast.8) | data formatting | bytes 786432
  80.2 2.0 %copy.18 = f32[192,1,512]{2,1,0:T(1,128)} copy(f32[192,1,512]{2,1,0:T(1,128)} %bitcast.7) | data formatting | bytes 786432
  82.2 1.9 %copy.19 = bf16[1,1,1,16,2,16,512]{6,5,4,3,2,1,0:T(8,128)(2,1)} copy(bf16[1,1,1,16,2,16,512]{6,5,4,3,2,1,0:T(8,128)(2,1)} %bitcast.6) | data formatting | bytes 1048576

commit v2 on v1

--- a/solution.py
+++ b/solution.py
@@ -25,15 +25,18 @@
     slices,
     hidden,
     out_grad,
-    block_list,
+    block_list_hbm,
     block_count,
     first,
     second,
+    changed_hbm,
+    placement_hbm,
+    first_out,
+    second_out,
+    pack_in,
+    block_list,
     changed,
     placement,
-    first_out,
-    second_out,
-    inbox,
     h_buf,
     g_buf,
     ht_buf,
@@ -44,10 +47,10 @@
     part_in,
     upd,
     pack,
-    pack_in,
     idx_vec,
     idx,
     load_sem,
+    small_sem,
     idx_sem,
     rs_send,
     rs_recv,
@@ -78,6 +81,18 @@
                 barrier, inc=1, device_id={"expert": me + off}, device_id_type=MESH
             )
 
+    small = [
+        pltpu.make_async_copy(src, dst, small_sem.at[i])
+        for i, (src, dst) in enumerate(
+            (
+                (changed_hbm, changed),
+                (placement_hbm, placement),
+                (block_list_hbm, block_list),
+            )
+        )
+    ]
+    for cp in small:
+        cp.start()
     groups = hidden_all // 512
     loads = [pltpu.make_async_copy(out_grad.at[0, 0], g_buf, load_sem.at[0])]
     for i in range(groups):
@@ -90,6 +105,8 @@
     for cp in loads:
         cp.start()
 
+    for cp in small:
+        cp.wait()
     lane = lax.broadcasted_iota(jnp.int32, (8, LANES), 1)
     owner_of = lane // SLOTS
     slot_of = lane - owner_of * SLOTS
@@ -125,6 +142,15 @@
             at = i * 512 + j * LANES
             ht_buf[pl.ds(at, LANES), :] = h_buf[:, pl.ds(at, LANES)].T
 
+    pl.semaphore_wait(barrier, n_dp - 1 + jnp.minimum(me, STRIDE))
+    for off in range(1, STRIDE + 1):
+
+        @pl.when(me - off >= 0)
+        def _():
+            pl.semaphore_signal(
+                near, inc=1, device_id={"expert": me - off}, device_id_type=MESH
+            )
+
     def reduce_copy(c, peer, slot):
         return pltpu.make_async_remote_copy(
             src_ref=part.at[c, peer],
@@ -143,15 +169,6 @@
                 preferred_element_type=jnp.float32,
             )
             part[c, d] = prod.astype(part.dtype)
-        if c == 0:
-            pl.semaphore_wait(barrier, n_dp - 1 + jnp.minimum(me, STRIDE))
-            for off in range(1, STRIDE + 1):
-
-                @pl.when(me - off >= 0)
-                def _():
-                    pl.semaphore_signal(
-                        near, inc=1, device_id={"expert": me - off}, device_id_type=MESH
-                    )
         for off in range(1, n_dp):
             reduce_copy(c, lax.rem(dp + off, n_dp), dp).start()
 
@@ -189,12 +206,15 @@
                 def _():
                     tell(sems.at[h + 1], onward)
 
-    def route_copy(c, peer, slot):
+    phases = ((0, 1), (1, 1), (2, chunks - 2))
+
+    def route_copy(p, peer, slot):
+        at = pl.ds(*phases[p])
         return pltpu.make_async_remote_copy(
-            src_ref=pack.at[c, peer],
-            dst_ref=pack_in.at[c, slot],
-            send_sem=z_send.at[c, peer],
-            recv_sem=z_recv.at[c, slot],
+            src_ref=pack.at[peer, at],
+            dst_ref=pack_in.at[slot, at],
+            send_sem=z_send.at[p, peer],
+            recv_sem=z_recv.at[p, slot],
             device_id={"expert": peer},
             device_id_type=MESH,
         )
@@ -218,21 +238,25 @@
         second_out[at, :] = jnp.where(keep, v_next, v_old)
         upd[pl.ds(0, slices)] = update.astype(upd.dtype).reshape(slices, slice_rows, LANES)
         for n in range(n_exp * SLOTS):
-            pack[c, n // SLOTS, n % SLOTS] = upd[idx[0, n]]
+            pack[n // SLOTS, c, n % SLOTS] = upd[idx[0, n]]
         if c == 0:
             learn(relay_left, me, me + STRIDE, me + STRIDE < n_exp)
+        done = [p for p, (start, size) in enumerate(phases) if start + size == c + 1]
+        if not done:
+            continue
+        p = done[0]
 
         @pl.loop(0, n_exp - 1)
         def _(i):
             @pl.when(i < me)
             def _():
-                route_copy(c, i, me).start()
+                route_copy(p, i, me).start()
 
         @pl.loop(1, STRIDE + 1)
         def _(off):
             @pl.when(me + off < n_exp)
             def _():
-                route_copy(c, me + off, me).start()
+                route_copy(p, me + off, me).start()
 
         if c == 0:
             learn(relay_right, n_exp - 1 - me, me - STRIDE, me - STRIDE >= 0)
@@ -241,25 +265,41 @@
         def _(off):
             @pl.when(me + off < n_exp)
             def _():
-                route_copy(c, me + off, me).start()
-
+                route_copy(p, me + off, me).start()
+
+    pack_in[me] = pack[me]
     for c in range(chunks):
-        cols = pl.ds(c * LANES, LANES)
-        inbox[me, :, :, cols] = pack[c, me]
+        for off in range(1, n_dp):
+            reduce_copy(c, lax.rem(dp + off, n_dp), dp).wait_send()
+    for p in range(len(phases)):
 
         @pl.loop(1, n_exp)
         def _(off):
             peer = lax.rem(me + off, n_exp)
-            route_copy(c, peer, peer).wait_recv()
-            inbox[peer, :, :, cols] = pack_in[c, peer]
-
+            route_copy(p, peer, me).wait_send()
+            route_copy(p, peer, peer).wait_recv()
+
+
+def store_kernel(first, second, pack, first_out, second_out, inbox, sem):
+    chunks = pack.shape[1]
+    copies = [
+        pltpu.make_async_copy(first, first_out, sem.at[0]),
+        pltpu.make_async_copy(second, second_out, sem.at[1]),
+    ]
     for c in range(chunks):
-        for off in range(1, n_dp):
-            reduce_copy(c, lax.rem(dp + off, n_dp), dp).wait_send()
-
-        @pl.loop(1, n_exp)
-        def _(off):
-            route_copy(c, lax.rem(me + off, n_exp), me).wait_send()
+        copies.append(
+            pltpu.make_async_copy(
+                pack.at[:, c], inbox.at[:, :, :, pl.ds(c * LANES, LANES)], sem.at[2 + c]
+            )
+        )
+    for cp in copies:
+        cp.start()
+    for cp in copies:
+        cp.wait()
+
+
+def in_hbm(x):
+    return pltpu.with_memory_space_constraint(x, pltpu.HBM)
 
 
 def on_device(
@@ -276,20 +316,23 @@
     flat = (rows * chunks, LANES)
     f32, bf16 = jnp.float32, jnp.bfloat16
     any_spec = pl.BlockSpec(memory_space=pltpu.HBM)
-    smem = pl.BlockSpec(memory_space=pltpu.SMEM)
     vmem = pl.BlockSpec(memory_space=pltpu.VMEM)
     dma = pltpu.SemaphoreType.DMA
     regular = pltpu.SemaphoreType.REGULAR
-    first_next, second_next, inbox = pl.pallas_call(
+    swapped = jnp.swapaxes(placement, 3, 4)
+    results = pl.pallas_call(
         functools.partial(kernel, n_dp, n_exp, slices),
         out_shape=(
-            jax.ShapeDtypeStruct(flat, f32),
-            jax.ShapeDtypeStruct(flat, f32),
-            jax.ShapeDtypeStruct((n_exp, SLOTS, slice_rows, features), bf16),
+            pltpu.VMEM(flat, f32),
+            pltpu.VMEM(flat, f32),
+            pltpu.VMEM((n_exp, chunks, SLOTS, slice_rows, LANES), bf16),
         ),
-        in_specs=[any_spec, any_spec, smem, smem, any_spec, any_spec, smem, smem],
+        in_specs=[any_spec] * 3 + [pl.BlockSpec(memory_space=pltpu.SMEM)] + [any_spec] * 4,
         out_specs=(vmem, vmem, vmem),
         scratch_shapes=[
+            pltpu.SMEM(block_list.shape, jnp.int32),
+            pltpu.SMEM(changed.shape, jnp.int32),
+            pltpu.SMEM(swapped.shape, jnp.int32),
             pltpu.VMEM((tokens, hidden_all), bf16),
             pltpu.VMEM((tokens, features), bf16),
             pltpu.VMEM((hidden_all, tokens), bf16),
@@ -299,33 +342,44 @@
             pltpu.VMEM((chunks, n_dp, rows, LANES), bf16),
             pltpu.VMEM((chunks, n_dp, rows, LANES), bf16),
             pltpu.VMEM((slices + 1, slice_rows, LANES), bf16),
-            pltpu.VMEM((chunks, n_exp, SLOTS, slice_rows, LANES), bf16),
-            pltpu.VMEM((chunks, n_exp, SLOTS, slice_rows, LANES), bf16),
+            pltpu.VMEM((n_exp, chunks, SLOTS, slice_rows, LANES), bf16),
             pltpu.VMEM((8, LANES), jnp.int32),
             pltpu.SMEM((8, LANES), jnp.int32),
             dma((3 + hidden_all // 512,)),
+            dma((3,)),
             dma(()),
             dma((chunks, n_dp)),
             dma((chunks, n_dp)),
-            dma((chunks, n_exp)),
-            dma((chunks, n_exp)),
+            dma((3, n_exp)),
+            dma((3, n_exp)),
             regular(()),
             regular((4,)),
             regular((4,)),
         ],
         compiler_params=pltpu.CompilerParams(
-            collective_id=0, has_side_effects=True, vmem_limit_bytes=60 << 20
+            collective_id=0, has_side_effects=True, vmem_limit_bytes=32 << 20
         ),
     )(
-        hidden,
-        out_grad,
-        block_list,
+        in_hbm(hidden),
+        in_hbm(out_grad),
+        in_hbm(block_list),
         block_count,
-        first_moment.reshape(flat),
-        second_moment.reshape(flat),
-        changed,
-        jnp.swapaxes(placement, 3, 4),
+        in_hbm(first_moment.reshape(flat)),
+        in_hbm(second_moment.reshape(flat)),
+        in_hbm(changed),
+        in_hbm(swapped),
     )
+    first_next, second_next, inbox = pl.pallas_call(
+        store_kernel,
+        out_shape=(
+            jax.ShapeDtypeStruct(flat, f32),
+            jax.ShapeDtypeStruct(flat, f32),
+            jax.ShapeDtypeStruct((n_exp, SLOTS, slice_rows, features), bf16),
+        ),
+        in_specs=[vmem] * 3,
+        out_specs=(any_spec,) * 3,
+        scratch_shapes=[dma((2 + chunks,))],
+    )(*(pltpu.with_memory_space_constraint(x, pltpu.VMEM) for x in results))
     shape = first_moment.shape
     return (
         first_next.reshape(shape),

time: 84.4 us -> 72 us (0.85)
  the two profiles are of different devices: /device:TPU:1 before, /device:TPU:32 now
where the time goes in v2:
time: 72 us; the launch traced here: 71.8 us
  Pallas kernels  70.5 us (98%)
  between operations  1.29 us (2%)
    pallas_call x1, Pallas kernels, on_device(): pl.pallas_call(functools.partial(kernel, n_dp, n_exp, slices), out_shape=...  69.4 us

profile of v2, /device:TPU:32, one launch (start us, length us, event | category | flops | bytes accessed | tf_op | source)
XLA Modules:
  0.0 71.8 jit_solution(10812033282825523398)
XLA Ops:
  1.3 69.4 %shard_map.103 = (f32[768,128]{1,0:T(8,128)S(1)}, f32[768,128]{1,0:T(8,128)S(1)}, bf16[16,4,2,16,128]{4,3,2,1,0:T(8,128)(2,1)S(1)}) custom-call(bf16[1,1,768,1536]{3,2,1,0:T(8,128)(2,1)} %hidden.1, bf16[1,1,768,512]{3,2,1,0:T(8,128)(2,1)} %out_grad.1, s32[1,1,6]{2,1,0:T(1,128)} %block_list_hbm.1, s32[1,1]{1,0:T(1,128)S(6)} %copy.13.block_count, ...), custom_call_target="tpu_custom_call" | custom-call | tf_op jit(solution)/shard_map/pallas_call | solution.py:323
  70.7 1.1 %shard_map.104 = (f32[768,128]{1,0:T(8,128)}, f32[768,128]{1,0:T(8,128)}, bf16[16,2,16,512]{3,2,1,0:T(8,128)(2,1)}) custom-call(f32[768,128]{1,0:T(8,128)S(1)} %get-tuple-element.9.first, f32[768,128]{1,0:T(8,128)S(1)} %get-tuple-element.10.second, bf16[16,4,2,16,128]{4,3,2,1,0:T(8,128)(2,1)S(1)} %get-tuple-element.11.pack), custom_call_target="tpu_custom_call" | custom-call | tf_op jit(solution)/shard_map/pallas_call | solution.py:372

commit v3 on v2

--- a/solution.py
+++ b/solution.py
@@ -11,7 +11,6 @@
 BLOCK = 128
 LANES = 128
 SLOTS = 2
-STRIDE = 5
 
 beta_one = 0.9
 beta_two = 0.95
@@ -44,6 +43,7 @@
     v_buf,
     keep_buf,
     part,
+    pair_in,
     part_in,
     upd,
     pack,
@@ -52,16 +52,20 @@
     load_sem,
     small_sem,
     idx_sem,
+    pair_send,
+    pair_recv,
     rs_send,
     rs_recv,
     z_send,
     z_recv,
-    near,
-    relay_left,
-    relay_right,
+    ready,
 ):
     dp = lax.axis_index("dp")
     me = lax.axis_index("expert")
+    pairs = n_dp // 2
+    place = dp // 2
+    side = dp - 2 * place
+    sibling = 2 * place + 1 - side
     tokens, hidden_all = h_buf.shape
     rows = hidden_all // n_dp
     slice_rows = rows // slices
@@ -69,12 +73,11 @@
     blocks = tokens // BLOCK
 
     barrier = pltpu.get_barrier_semaphore()
-    for off in range(1, n_dp):
-        pl.semaphore_signal(
-            barrier, inc=1, device_id={"dp": lax.rem(dp + off, n_dp)}, device_id_type=MESH
-        )
-    for off in range(1, STRIDE + 1):
-
+    for peer in [sibling] + [2 * lax.rem(place + off, pairs) + side for off in range(1, pairs)]:
+        pl.semaphore_signal(barrier, inc=1, device_id={"dp": peer}, device_id_type=MESH)
+
+    @pl.loop(1, n_exp)
+    def _(off):
         @pl.when(me + off < n_exp)
         def _():
             pl.semaphore_signal(
@@ -107,6 +110,76 @@
 
     for cp in small:
         cp.wait()
+    loads[0].wait()
+    for b in range(blocks):
+        live = jnp.int32(0)
+        for j in range(blocks):
+            hit = (block_list[0, 0, j] == b) & (block_count[0, 0] > j)
+            live = live | hit.astype(jnp.int32)
+        at = pl.ds(b * BLOCK, BLOCK)
+        block = g_buf[at, :]
+        g_buf[at, :] = jnp.where(live > 0, block, jnp.zeros_like(block))
+    for i in range(groups):
+        loads[1 + i].wait()
+        for j in range(512 // LANES):
+            at = i * 512 + j * LANES
+            ht_buf[pl.ds(at, LANES), :] = h_buf[:, pl.ds(at, LANES)].T
+
+    def pair_copy(c):
+        return pltpu.make_async_remote_copy(
+            src_ref=part.at[c, 1 - side],
+            dst_ref=pair_in.at[c],
+            send_sem=pair_send.at[c],
+            recv_sem=pair_recv.at[c],
+            device_id={"dp": sibling},
+            device_id_type=MESH,
+        )
+
+    def reduce_copy(c, peer, slot):
+        return pltpu.make_async_remote_copy(
+            src_ref=part.at[c, side, peer],
+            dst_ref=part_in.at[c, slot],
+            send_sem=rs_send.at[c, peer],
+            recv_sem=rs_recv.at[c, slot],
+            device_id={"dp": 2 * peer + side},
+            device_id_type=MESH,
+        )
+
+    def enter():
+        pl.semaphore_wait(barrier, pairs + me)
+
+        @pl.loop(1, n_exp)
+        def _(off):
+            @pl.when(me - off >= 0)
+            def _():
+                pl.semaphore_signal(
+                    ready.at[me], inc=1, device_id={"expert": me - off}, device_id_type=MESH
+                )
+
+    def multiply(c):
+        width = 2 * LANES
+        for d in range(n_dp):
+            prod = jnp.dot(
+                ht_buf[pl.ds(d * rows, rows), :],
+                g_buf[:, pl.ds(c * LANES, width)],
+                preferred_element_type=jnp.float32,
+            ).astype(part.dtype)
+            part[c, d % 2, d // 2] = prod[:, :LANES]
+            part[c + 1, d % 2, d // 2] = prod[:, LANES:]
+        if c == 0:
+            enter()
+        pair_copy(c).start()
+        pair_copy(c + 1).start()
+
+    def add_pair(c):
+        pair_copy(c).wait_recv()
+        mine = part[c, side].astype(jnp.float32) + pair_in[c].astype(jnp.float32)
+        part[c, side] = mine.astype(part.dtype)
+        for off in range(1, pairs):
+            reduce_copy(c, lax.rem(place + off, pairs), place).start()
+
+    multiply(0)
+
     lane = lax.broadcasted_iota(jnp.int32, (8, LANES), 1)
     owner_of = lane // SLOTS
     slot_of = lane - owner_of * SLOTS
@@ -127,86 +200,16 @@
         )
     upd[slices] = jnp.zeros(upd.shape[1:], upd.dtype)
 
-    loads[0].wait()
-    for b in range(blocks):
-        live = jnp.int32(0)
-        for j in range(blocks):
-            hit = (block_list[0, 0, j] == b) & (block_count[0, 0] > j)
-            live = live | hit.astype(jnp.int32)
-        at = pl.ds(b * BLOCK, BLOCK)
-        block = g_buf[at, :]
-        g_buf[at, :] = jnp.where(live > 0, block, jnp.zeros_like(block))
-    for i in range(groups):
-        loads[1 + i].wait()
-        for j in range(512 // LANES):
-            at = i * 512 + j * LANES
-            ht_buf[pl.ds(at, LANES), :] = h_buf[:, pl.ds(at, LANES)].T
-
-    pl.semaphore_wait(barrier, n_dp - 1 + jnp.minimum(me, STRIDE))
-    for off in range(1, STRIDE + 1):
-
-        @pl.when(me - off >= 0)
-        def _():
-            pl.semaphore_signal(
-                near, inc=1, device_id={"expert": me - off}, device_id_type=MESH
-            )
-
-    def reduce_copy(c, peer, slot):
-        return pltpu.make_async_remote_copy(
-            src_ref=part.at[c, peer],
-            dst_ref=part_in.at[c, slot],
-            send_sem=rs_send.at[c, peer],
-            recv_sem=rs_recv.at[c, slot],
-            device_id={"dp": peer},
-            device_id_type=MESH,
-        )
-
-    for c in range(chunks):
-        for d in range(n_dp):
-            prod = jnp.dot(
-                ht_buf[pl.ds(d * rows, rows), :],
-                g_buf[:, pl.ds(c * LANES, LANES)],
-                preferred_element_type=jnp.float32,
-            )
-            part[c, d] = prod.astype(part.dtype)
-        for off in range(1, n_dp):
-            reduce_copy(c, lax.rem(dp + off, n_dp), dp).start()
+    add_pair(0)
+    multiply(2)
+    add_pair(1)
 
     loads[1 + groups].wait()
     loads[2 + groups].wait()
     idx_copy.wait()
 
-    def tell(sem, peer):
-        pl.semaphore_signal(sem, inc=1, device_id={"expert": peer}, device_id_type=MESH)
-
-    @pl.when(me + 1 < n_exp)
-    def _():
-        pl.semaphore_wait(near, jnp.minimum(n_exp - 1 - me, STRIDE))
-
-    @pl.when((me + STRIDE < n_exp) & (me > 0))
-    def _():
-        tell(relay_left.at[0], me + STRIDE)
-
-    @pl.when((me - STRIDE >= 0) & (me + 1 < n_exp))
-    def _():
-        tell(relay_right.at[0], me - STRIDE)
-
-    hops = -(-(n_exp - 1) // STRIDE) - 1
-
-    def learn(sems, reach, onward, far_enough):
-        for h in range(hops):
-
-            @pl.when(reach > (h + 1) * STRIDE)
-            def _():
-                pl.semaphore_wait(sems.at[h], 1)
-
-            if h + 1 < hops:
-
-                @pl.when(far_enough & (reach > (h + 1) * STRIDE))
-                def _():
-                    tell(sems.at[h + 1], onward)
-
-    phases = ((0, 1), (1, 1), (2, chunks - 2))
+    phases = ((0, 1), (1, chunks - 1), (0, chunks))
+    middle = 5 * n_exp // 8
 
     def route_copy(p, peer, slot):
         at = pl.ds(*phases[p])
@@ -219,14 +222,64 @@
             device_id_type=MESH,
         )
 
+    def far_first(low, high, act):
+        @pl.loop(0, high - low)
+        def _(i):
+            act(high - 1 - i)
+
+    def send_left(p):
+        def act(off):
+            @pl.when(me - off >= 0)
+            def _():
+                route_copy(p, me - off, me).start()
+
+        return act
+
+    def send_right(p):
+        def act(off):
+            @pl.when(me + off < n_exp)
+            def _():
+                if p != 1:
+                    pl.semaphore_wait(ready.at[me + off], 1)
+                route_copy(p, me + off, me).start()
+
+        return act
+
+    def wait_sent(p):
+        def act(off):
+            @pl.when(me - off >= 0)
+            def _():
+                route_copy(p, me - off, me).wait_send()
+
+            @pl.when(me + off < n_exp)
+            def _():
+                route_copy(p, me + off, me).wait_send()
+
+        return act
+
+    def wait_received(p):
+        def act(off):
+            @pl.when(me - off >= 0)
+            def _():
+                route_copy(p, me - off, me - off).wait_recv()
+
+            @pl.when(me + off < n_exp)
+            def _():
+                route_copy(p, me + off, me + off).wait_recv()
+
+        return act
+
     corr_one = 1.0 - beta_one**step_number
     corr_two = 1.0 - beta_two**step_number
     for c in range(chunks):
-        total = part[c, dp].astype(jnp.float32)
-        for off in range(1, n_dp):
-            peer = lax.rem(dp + off, n_dp)
+        total = part[c, side, place].astype(jnp.float32)
+        for off in range(1, pairs):
+            peer = lax.rem(place + off, pairs)
             reduce_copy(c, peer, peer).wait_recv()
             total = total + part_in[c, peer].astype(jnp.float32)
+        if c == 0:
+            add_pair(2)
+            add_pair(3)
         at = pl.ds(c, rows, stride=chunks)
         m_old = m_buf[at, :]
         v_old = v_buf[at, :]
@@ -240,44 +293,24 @@
         for n in range(n_exp * SLOTS):
             pack[n // SLOTS, c, n % SLOTS] = upd[idx[0, n]]
         if c == 0:
-            learn(relay_left, me, me + STRIDE, me + STRIDE < n_exp)
-        done = [p for p, (start, size) in enumerate(phases) if start + size == c + 1]
-        if not done:
-            continue
-        p = done[0]
-
-        @pl.loop(0, n_exp - 1)
-        def _(i):
-            @pl.when(i < me)
-            def _():
-                route_copy(p, i, me).start()
-
-        @pl.loop(1, STRIDE + 1)
-        def _(off):
-            @pl.when(me + off < n_exp)
-            def _():
-                route_copy(p, me + off, me).start()
-
-        if c == 0:
-            learn(relay_right, n_exp - 1 - me, me - STRIDE, me - STRIDE >= 0)
-
-        @pl.loop(STRIDE + 1, n_exp)
-        def _(off):
-            @pl.when(me + off < n_exp)
-            def _():
-                route_copy(p, me + off, me).start()
+            far_first(1, middle + 1, send_left(0))
+            pl.loop(1, middle + 1)(send_right(0))
+
+    far_first(middle + 1, n_exp, send_left(2))
+    far_first(1, middle + 1, send_left(1))
+    pl.loop(middle + 1, n_exp)(send_right(2))
+    far_first(1, middle + 1, send_right(1))
 
     pack_in[me] = pack[me]
     for c in range(chunks):
-        for off in range(1, n_dp):
-            reduce_copy(c, lax.rem(dp + off, n_dp), dp).wait_send()
-    for p in range(len(phases)):
-
-        @pl.loop(1, n_exp)
-        def _(off):
-            peer = lax.rem(me + off, n_exp)
-            route_copy(p, peer, me).wait_send()
-            route_copy(p, peer, peer).wait_recv()
+        pair_copy(c).wait_send()
+        for off in range(1, pairs):
+            reduce_copy(c, lax.rem(place + off, pairs), place).wait_send()
+    for p in (0, 1):
+        far_first(1, middle + 1, wait_sent(p))
+        far_first(1, middle + 1, wait_received(p))
+    far_first(middle + 1, n_exp, wait_sent(2))
+    far_first(middle + 1, n_exp, wait_received(2))
 
 
 def store_kernel(first, second, pack, first_out, second_out, inbox, sem):
@@ -339,8 +372,9 @@
             pltpu.VMEM(flat, f32),
             pltpu.VMEM(flat, f32),
             pltpu.VMEM((rows, LANES), jnp.int32),
-            pltpu.VMEM((chunks, n_dp, rows, LANES), bf16),
-            pltpu.VMEM((chunks, n_dp, rows, LANES), bf16),
+            pltpu.VMEM((chunks, 2, n_dp // 2, rows, LANES), bf16),
+            pltpu.VMEM((chunks, n_dp // 2, rows, LANES), bf16),
+            pltpu.VMEM((chunks, n_dp // 2, rows, LANES), bf16),
             pltpu.VMEM((slices + 1, slice_rows, LANES), bf16),
             pltpu.VMEM((n_exp, chunks, SLOTS, slice_rows, LANES), bf16),
             pltpu.VMEM((8, LANES), jnp.int32),
@@ -348,13 +382,13 @@
             dma((3 + hidden_all // 512,)),
             dma((3,)),
             dma(()),
-            dma((chunks, n_dp)),
-            dma((chunks, n_dp)),
+            dma((chunks,)),
+            dma((chunks,)),
+            dma((chunks, n_dp // 2)),
+            dma((chunks, n_dp // 2)),
             dma((3, n_exp)),
             dma((3, n_exp)),
-            regular(()),
-            regular((4,)),
-            regular((4,)),
+            regular((n_exp,)),
         ],
         compiler_params=pltpu.CompilerParams(
             collective_id=0, has_side_effects=True, vmem_limit_bytes=32 << 20

time: 72 us -> 69.2 us (0.961)
  the two profiles are of different devices: /device:TPU:32 before, /device:TPU:161 now
where the time goes in v3:
time: 69.2 us; the launch traced here: 69 us
  Pallas kernels  67.8 us (98%)
  between operations  1.29 us (2%)
    pallas_call x1, Pallas kernels, on_device(): pl.pallas_call(functools.partial(kernel, n_dp, n_exp, slices), out_shape=...  66.7 us

profile of v3, /device:TPU:161, one launch (start us, length us, event | category | flops | bytes accessed | tf_op | source)
XLA Modules:
  0.0 69.0 jit_solution(9453199985745980890)
XLA Ops:
  1.3 66.7 %shard_map.103 = (f32[768,128]{1,0:T(8,128)S(1)}, f32[768,128]{1,0:T(8,128)S(1)}, bf16[16,4,2,16,128]{4,3,2,1,0:T(8,128)(2,1)S(1)}) custom-call(bf16[1,1,768,1536]{3,2,1,0:T(8,128)(2,1)} %hidden.1, bf16[1,1,768,512]{3,2,1,0:T(8,128)(2,1)} %out_grad.1, s32[1,1,6]{2,1,0:T(1,128)} %block_list_hbm.1, s32[1,1]{1,0:T(1,128)S(6)} %copy.13.block_count, ...), custom_call_target="tpu_custom_call" | custom-call | tf_op jit(solution)/shard_map/pallas_call | solution.py:356
  67.9 1.1 %shard_map.104 = (f32[768,128]{1,0:T(8,128)}, f32[768,128]{1,0:T(8,128)}, bf16[16,2,16,512]{3,2,1,0:T(8,128)(2,1)}) custom-call(f32[768,128]{1,0:T(8,128)S(1)} %get-tuple-element.9.first, f32[768,128]{1,0:T(8,128)S(1)} %get-tuple-element.10.second, bf16[16,4,2,16,128]{4,3,2,1,0:T(8,128)(2,1)S(1)} %get-tuple-element.11.pack), custom_call_target="tpu_custom_call" | custom-call | tf_op jit(solution)/shard_map/pallas_call | solution.py:406

commit v4 on v3

--- a/solution.py
+++ b/solution.py
@@ -76,13 +76,19 @@
     for peer in [sibling] + [2 * lax.rem(place + off, pairs) + side for off in range(1, pairs)]:
         pl.semaphore_signal(barrier, inc=1, device_id={"dp": peer}, device_id_type=MESH)
 
-    @pl.loop(1, n_exp)
-    def _(off):
-        @pl.when(me + off < n_exp)
-        def _():
-            pl.semaphore_signal(
-                barrier, inc=1, device_id={"expert": me + off}, device_id_type=MESH
-            )
+    @pl.when(me == 0)
+    def _():
+        pl.semaphore_signal(barrier, inc=1, device_id={"expert": 1}, device_id_type=MESH)
+
+    @pl.when(me > 0)
+    def _():
+        @pl.loop(1, n_exp)
+        def _(off):
+            @pl.when(me + off < n_exp)
+            def _():
+                pl.semaphore_signal(
+                    barrier, inc=1, device_id={"expert": me + off}, device_id_type=MESH
+                )
 
     small = [
         pltpu.make_async_copy(src, dst, small_sem.at[i])
@@ -105,7 +111,7 @@
         )
     loads.append(pltpu.make_async_copy(first, m_buf, load_sem.at[1 + groups]))
     loads.append(pltpu.make_async_copy(second, v_buf, load_sem.at[2 + groups]))
-    for cp in loads:
+    for cp in loads[: 1 + groups]:
         cp.start()
 
     for cp in small:
@@ -145,16 +151,19 @@
             device_id_type=MESH,
         )
 
+    def tell(who, peer):
+        pl.semaphore_signal(
+            ready.at[who], inc=1, device_id={"expert": peer}, device_id_type=MESH
+        )
+
     def enter():
-        pl.semaphore_wait(barrier, pairs + me)
-
-        @pl.loop(1, n_exp)
-        def _(off):
-            @pl.when(me - off >= 0)
-            def _():
-                pl.semaphore_signal(
-                    ready.at[me], inc=1, device_id={"expert": me - off}, device_id_type=MESH
-                )
+        pl.semaphore_wait(barrier, pairs + jnp.where(me == 1, 1, jnp.maximum(me - 1, 0)))
+
+        @pl.loop(0, n_exp - 1)
+        def _(peer):
+            @pl.when((peer < me) & ((peer > 0) | (me == 1)))
+            def _():
+                tell(me, peer)
 
     def multiply(c):
         width = 2 * LANES
@@ -175,10 +184,12 @@
         pair_copy(c).wait_recv()
         mine = part[c, side].astype(jnp.float32) + pair_in[c].astype(jnp.float32)
         part[c, side] = mine.astype(part.dtype)
-        for off in range(1, pairs):
+        for off in (2, 1, 3):
             reduce_copy(c, lax.rem(place + off, pairs), place).start()
 
     multiply(0)
+    for cp in loads[1 + groups :]:
+        cp.start()
 
     lane = lax.broadcasted_iota(jnp.int32, (8, LANES), 1)
     owner_of = lane // SLOTS
@@ -229,7 +240,7 @@
 
     def send_left(p):
         def act(off):
-            @pl.when(me - off >= 0)
+            @pl.when(me - off > 0)
             def _():
                 route_copy(p, me - off, me).start()
 
@@ -240,14 +251,20 @@
             @pl.when(me + off < n_exp)
             def _():
                 if p != 1:
+
                     pl.semaphore_wait(ready.at[me + off], 1)
+
+                    @pl.when(me == 1)
+                    def _():
+                        tell(0, me + off)
+
                 route_copy(p, me + off, me).start()
 
         return act
 
     def wait_sent(p):
         def act(off):
-            @pl.when(me - off >= 0)
+            @pl.when(me - off > 0)
             def _():
                 route_copy(p, me - off, me).wait_send()
 
@@ -263,7 +280,7 @@
             def _():
                 route_copy(p, me - off, me - off).wait_recv()
 
-            @pl.when(me + off < n_exp)
+            @pl.when((me > 0) & (me + off < n_exp))
             def _():
                 route_copy(p, me + off, me + off).wait_recv()
 
@@ -297,6 +314,15 @@
             pl.loop(1, middle + 1)(send_right(0))
 
     far_first(middle + 1, n_exp, send_left(2))
+    @pl.when(me > 1)
+    def _():
+        pl.semaphore_wait(ready.at[0], 1)
+        tell(me, 0)
+
+    @pl.when(me > 0)
+    def _():
+        route_copy(2, 0, me).start()
+
     far_first(1, middle + 1, send_left(1))
     pl.loop(middle + 1, n_exp)(send_right(2))
     far_first(1, middle + 1, send_right(1))
@@ -306,11 +332,22 @@
         pair_copy(c).wait_send()
         for off in range(1, pairs):
             reduce_copy(c, lax.rem(place + off, pairs), place).wait_send()
-    for p in (0, 1):
-        far_first(1, middle + 1, wait_sent(p))
-        far_first(1, middle + 1, wait_received(p))
+    far_first(1, middle + 1, wait_sent(0))
+    far_first(1, middle + 1, wait_sent(1))
     far_first(middle + 1, n_exp, wait_sent(2))
+    far_first(1, middle + 1, wait_received(0))
     far_first(middle + 1, n_exp, wait_received(2))
+    far_first(1, middle + 1, wait_received(1))
+
+    @pl.when(me > 0)
+    def _():
+        route_copy(2, 0, me).wait_send()
+
+    @pl.when(me == 0)
+    def _():
+        @pl.loop(1, n_exp)
+        def _(peer):
+            route_copy(2, peer, peer).wait_recv()
 
 
 def store_kernel(first, second, pack, first_out, second_out, inbox, sem):

time: 69.2 us -> 67.5 us (0.975)
  the two profiles are of different devices: /device:TPU:161 before, /device:TPU:168 now
where the time goes in v4:
time: 67.5 us; the launch traced here: 67.3 us
  Pallas kernels  66 us (98%)
  between operations  1.29 us (2%)
    pallas_call x1, Pallas kernels, on_device(): pl.pallas_call(functools.partial(kernel, n_dp, n_exp, slices), out_shape=...  64.9 us

profile of v4, /device:TPU:168, one launch (start us, length us, event | category | flops | bytes accessed | tf_op | source)
XLA Modules:
  0.0 67.3 jit_solution(971399319795156821)
XLA Ops:
  1.3 64.9 %shard_map.103 = (f32[768,128]{1,0:T(8,128)S(1)}, f32[768,128]{1,0:T(8,128)S(1)}, bf16[16,4,2,16,128]{4,3,2,1,0:T(8,128)(2,1)S(1)}) custom-call(bf16[1,1,768,1536]{3,2,1,0:T(8,128)(2,1)} %hidden.1, bf16[1,1,768,512]{3,2,1,0:T(8,128)(2,1)} %out_grad.1, s32[1,1,6]{2,1,0:T(1,128)} %block_list_hbm.1, s32[1,1]{1,0:T(1,128)S(6)} %copy.13.block_count, ...), custom_call_target="tpu_custom_call" | custom-call | tf_op jit(solution)/shard_map/pallas_call | solution.py:393
  66.2 1.1 %shard_map.104 = (f32[768,128]{1,0:T(8,128)}, f32[768,128]{1,0:T(8,128)}, bf16[16,2,16,512]{3,2,1,0:T(8,128)(2,1)}) custom-call(f32[768,128]{1,0:T(8,128)S(1)} %get-tuple-element.9.first, f32[768,128]{1,0:T(8,128)S(1)} %get-tuple-element.10.second, bf16[16,4,2,16,128]{4,3,2,1,0:T(8,128)(2,1)S(1)} %get-tuple-element.11.pack), custom_call_target="tpu_custom_call" | custom-call | tf_op jit(solution)/shard_map/pallas_call | solution.py:443
